TPU v7x, 128 devices: a whole 4x4x4 slice. The times are simulated.
128 devices in a mesh: row: 16 (over z, x_lo, core), col: 8 (over x_hi, y).
Axes of the slice: x: 4 (x_hi: 2, x_lo: 2; x = x_hi * 2 + x_lo), y: 4, z: 4, core: 2. Of those that a mesh axis runs over, the one named last changes fastest.
Arguments:
- tile_values: bfloat16 [32768, 128, 128], P(('row', 'col')), may hold values from -0.09375 to 0.09375
- slot_codes: int32 [32768], P(('row', 'col')), may hold values from -1 to 511, as said below
- right_start: float32 [32768, 256], P(('row', 'col')), may hold values from -6 to 6
- left_start: float32 [32768, 256], P(('row', 'col')), may hold values from -6 to 6
- node_diagonal: float32 [32768], P(('row', 'col')), may hold values from 1 to 3
- row_scale: float32 [32768], P(('row', 'col')), may hold values from 0.2 to 15
Outputs:
- right_block: float32 [32768, 256], P(('row', 'col'))
- left_block: float32 [32768, 256], P(('row', 'col'))
- projections: float32 [2, 256, 256], replicated
Inputs may be any that keep to these rules, and one draw needn't show every extreme that they name: `slot_codes`: slot (s, p, c) carries a tile that device s extracted for owner p; its code is -1 (empty) or a position a 32 + b in p's block grid of 16 x 2 * 16 places. The codes of one owner's live slots over all sources are distinct, so an owner receives at most 128 live tiles, and some owner receives exactly 128. A source fills at most 2 slots for one owner, and some source fills all 2.
All inputs are finite; a program needn't handle non-finite values.
Results may differ from a plain program's by a relative error of at most 0.002.
Values may be sent and summed in bfloat16 or wider, within the bound.
A program may use at most 128 MiB of HBM per device.

v0:
```python
import jax
import jax.numpy as jnp
from jax import lax
from jax.sharding import PartitionSpec as P

ITERS = 2
epsilon = 1e-06


def slot_product(slot_tiles, pick_keys, sum_keys, blocks, key_count, transposed):
    tile_rows = slot_tiles.shape[1]
    port_count = blocks.shape[2]
    slot_total = slot_tiles.shape[0]
    groups = 4
    grouped_tiles = slot_tiles.reshape(groups, slot_total // groups, tile_rows, tile_rows)
    grouped_pick = pick_keys.reshape(groups, slot_total // groups)
    grouped_sum = sum_keys.reshape(groups, slot_total // groups)
    form = "syx,syp->sxp" if transposed else "sxy,syp->sxp"

    def accumulate(summed, group):
        group_tiles, group_pick, group_sum = group
        picked = blocks[group_pick]
        contrib = jnp.einsum(form, group_tiles, picked, preferred_element_type=jnp.float32)
        onehot = (group_sum[:, None] == jnp.arange(key_count)[None, :]).astype(jnp.float32)
        added = jnp.einsum("sn,sxp->nxp", onehot, contrib, precision=lax.Precision.HIGHEST)
        return (summed + added, None)

    start = jnp.zeros((key_count, tile_rows, port_count), jnp.float32)
    summed, _ = lax.scan(accumulate, start, (grouped_tiles, grouped_pick, grouped_sum))
    return summed.reshape(key_count * tile_rows, port_count)


def local(tile_values, slot_codes, right_start, left_start, node_diagonal, row_scale):
    row_size = lax.axis_size("row")
    col_size = lax.axis_size("col")
    owners = row_size * col_size
    tile_rows = tile_values.shape[1]
    port_count = right_start.shape[1]
    order_rows = right_start.shape[0] * owners
    grid_rows = 2 * col_size
    grid_cols = 2 * row_size
    got_tiles, got_codes = (
        lax.all_to_all(tile_values, ("row", "col"), split_axis=0, concat_axis=0, tiled=True),
        lax.all_to_all(slot_codes, ("row", "col"), split_axis=0, concat_axis=0, tiled=True),
    )
    live = got_codes >= 0
    block_row = got_codes // grid_cols
    block_col = got_codes % grid_cols
    row_sum_key = jnp.where(live, block_row, grid_rows)
    col_pick_key = jnp.where(live, block_col, 0)
    row_pick_key = jnp.where(live, block_row, 0)
    col_sum_key = jnp.where(live, block_col, grid_cols)
    scale_col = row_scale[:, None]
    diag_col = node_diagonal[:, None]
    right_vec = right_start
    left_vec = right_start + left_start
    stored = []
    for turn in range(ITERS):
        right_bf = right_vec.astype(jnp.bfloat16)
        scaled_left = scale_col * left_vec
        left_bf = scaled_left.astype(jnp.bfloat16)
        right_cols = lax.all_gather(right_bf, "row", axis=0, tiled=True)
        left_rows = lax.all_gather(left_bf, "col", axis=0, tiled=True)
        right_blocks = right_cols.reshape(grid_cols, tile_rows, port_count)
        right_part = slot_product(
            got_tiles, col_pick_key, row_sum_key, right_blocks, grid_rows, False
        )
        blocks = left_rows.reshape(grid_rows, tile_rows, port_count)
        left_part = slot_product(got_tiles, row_pick_key, col_sum_key, blocks, grid_cols, True)
        right_prod = lax.psum_scatter(right_part, "col", scatter_dimension=0, tiled=True)
        left_prod = lax.psum_scatter(left_part, "row", scatter_dimension=0, tiled=True)
        right_new = scale_col * (right_prod + diag_col * right_vec)
        left_new = left_prod + diag_col * scaled_left
        local_proj = jnp.dot(left_vec.T, right_new, precision=lax.Precision.HIGHEST)
        project = lax.psum(local_proj, ("row", "col")) / order_rows
        right_rest = right_new - jnp.dot(right_vec, project, precision=lax.Precision.HIGHEST)
        left_rest = left_new - jnp.dot(left_vec, project.T, precision=lax.Precision.HIGHEST)
        right_sq, left_sq = lax.psum(
            (jnp.sum(right_rest * right_rest, axis=0), jnp.sum(left_rest * left_rest, axis=0)),
            ("row", "col"),
        )
        right_vec = right_rest / jnp.sqrt(right_sq / order_rows + epsilon)[None, :]
        left_vec = left_rest / jnp.sqrt(left_sq / order_rows + epsilon)[None, :]
        stored.append(project)
    return (right_vec, left_vec, jnp.stack(stored))


def solution(mesh):
    return jax.shard_map(
        local,
        mesh=mesh,
        in_specs=(
            P(("row", "col"), None, None),
            P(("row", "col")),
            P(("row", "col"), None),
            P(("row", "col"), None),
            P(("row", "col")),
            P(("row", "col")),
        ),
        out_specs=(P(("row", "col"), None), P(("row", "col"), None), P()),
        check_vma=False,
    )
```

profile of v0, /device:TPU:1, one launch (start us, length us, event | category | flops | bytes accessed | tf_op | source)
XLA Modules:
  0.0 1186.2 jit_solution(6084935444073180689)
XLA Ops:
  8.0 21.1 %all_to_all.17 = s32[128,2,1]{1,2,0:T(1,128)S(1)} all-to-all(s32[128,2,1]{1,2,0:T(1,128)S(1)} %bitcast.149), channel_id=1, replica_groups=mesh['row'=16,'col'=8] {'row','col'}, dimensions={0} | all-to-all | bytes 2048 | tf_op jit(solution)/shard_map/all_to_all | solution.py:44
  29.1 5.3 all-to-all-start.1
  36.8 112.9 %all-gather.5.cloned.1.call-done = bf16[4096,256]{1,0:T(8,128)(2,1)} async-done(((bf16[256,256]{1,0:T(8,128)(2,1)}), bf16[4096,256]{1,0:T(8,128)(2,1)}) %all-gather.5.cloned.1.call-update) | async-done | bytes 2097168 | tf_op jit(solution)/shard_map/all_gather | solution.py:62
  149.7 90.1 %while.44 = (s32[]{:T(128)}, f32[16,128,256]{2,0,1:T(8,128)S(1)}, s32[4,64]{1,0:T(4,128)S(1)}, bf16[4,64,128,128]{3,2,1,0:T(8,128)(2,1)}, s32[4,64]{1,0:T(4,128)...) while((s32[]{:T(128)}, f32[16,128,256]{2,0,1:T(8,128)S(1)}, ...), condition=%wide.region_1.2_spmd.clone, body=%wide.region_0.1_spmd.clone.sunk | while | flops 940574912 | bytes 35658084 | solution.py:29
  149.7 4.3 gather_fusion
  154.1 7.3 fusion.117
  161.3 10.8 select_add_fusion.8
  172.2 4.3 gather_fusion
  176.6 7.3 fusion.117
  183.9 10.8 select_add_fusion.8
  194.8 4.3 gather_fusion
  199.1 7.3 fusion.117
  206.4 10.8 select_add_fusion.8
  217.3 4.3 gather_fusion
  221.6 7.3 fusion.117
  228.9 10.8 select_add_fusion.8
  243.1 12.0 %copy.22 = bf16[256,128,128]{1,2,0:T(8,128)(2,1)} copy(bf16[256,128,128]{2,1,0:T(8,128)(2,1)} %all-to-all-done.1) | data formatting | bytes 16777216 | tf_op jit(solution)/shard_map/all_to_all | solution.py:43
  255.1 61.6 %reduce-scatter.5.cloned.1.call-done = f32[256,256]{1,0:T(8,128)} async-done(((f32[2048,256]{1,0:T(8,128)}), f32[256,256]{1,0:T(8,128)}) %reduce-scatter.5.cloned.1.call-update) | async-done | bytes 262160 | tf_op jit(solution)/shard_map/reduce_scatter | solution.py:70
  319.7 45.1 %all-gather.9.cloned.1.call-done = bf16[2048,256]{1,0:T(8,128)(2,1)} async-done(((bf16[256,256]{1,0:T(8,128)(2,1)}), bf16[2048,256]{1,0:T(8,128)(2,1)}) %all-gather.9.cloned.1.call-update) | async-done | bytes 1048592 | tf_op jit(solution)/shard_map/all_gather | solution.py:63
  364.8 101.9 %while.46 = (s32[]{:T(128)}, f32[32,128,256]{2,0,1:T(8,128)}, s32[4,64]{1,0:T(4,128)S(1)}, bf16[4,64,128,128]{2,3,1,0:T(8,128)(2,1)}, s32[4,64]{1,0:T(4,128)S(1)...) while((s32[]{:T(128)}, f32[32,128,256]{2,0,1:T(8,128)}, s32[4,64]{1,0:T(4,128)S(1)}, ...), condition=%wide.region_10.11_spmd.clone, body=%wide.region_9.10_spmd.clone.sunk | while | flops 1344277760 | bytes 39852388 | solution.py:29
  368.8 7.3 fusion.131
  376.1 13.3 %select_add_fusion.10 = f32[32,128,256]{2,0,1:T(8,128)} fusion(f32[32,128,256]{2,0,1:T(8,128)} %get-tuple-element.481, f32[64,128,256]{2,1,0:T(8,128)} %fusion.131, pred[]{:T(512)S(6)} %compare.21, s32[64]{0:T(128)S(1)} %fusion.132), kind=kOutput, calls=%fused_computation.40.clone.1 | convolution fusion | flops 807405568 | bytes 16777472 | tf_op jit(solution)/shard_map/while/body/eval_jaxpr/sn,sxp->nxp/dot_general | solution.py:25
  393.4 7.3 fusion.131
  400.7 14.4 %select_add_fusion.10 = f32[32,128,256]{2,0,1:T(8,128)} fusion(f32[32,128,256]{2,0,1:T(8,128)} %get-tuple-element.481, f32[64,128,256]{2,1,0:T(8,128)} %fusion.131, pred[]{:T(512)S(6)} %compare.21, s32[64]{0:T(128)S(1)} %fusion.132), kind=kOutput, calls=%fused_computation.40.clone.1 | convolution fusion | flops 807405568 | bytes 16777472 | tf_op jit(solution)/shard_map/while/body/eval_jaxpr/sn,sxp->nxp/dot_general | solution.py:25
  419.1 7.3 fusion.131
  426.4 14.4 %select_add_fusion.10 = f32[32,128,256]{2,0,1:T(8,128)} fusion(f32[32,128,256]{2,0,1:T(8,128)} %get-tuple-element.481, f32[64,128,256]{2,1,0:T(8,128)} %fusion.131, pred[]{:T(512)S(6)} %compare.21, s32[64]{0:T(128)S(1)} %fusion.132), kind=kOutput, calls=%fused_computation.40.clone.1 | convolution fusion | flops 807405568 | bytes 16777472 | tf_op jit(solution)/shard_map/while/body/eval_jaxpr/sn,sxp->nxp/dot_general | solution.py:25
  444.8 7.3 fusion.131
  452.1 14.4 %select_add_fusion.10 = f32[32,128,256]{2,0,1:T(8,128)} fusion(f32[32,128,256]{2,0,1:T(8,128)} %get-tuple-element.481, f32[64,128,256]{2,1,0:T(8,128)} %fusion.131, pred[]{:T(512)S(6)} %compare.21, s32[64]{0:T(128)S(1)} %fusion.132), kind=kOutput, calls=%fused_computation.40.clone.1 | convolution fusion | flops 807405568 | bytes 16777472 | tf_op jit(solution)/shard_map/while/body/eval_jaxpr/sn,sxp->nxp/dot_general | solution.py:25
  466.7 6.6 copy.27
  473.4 38.5 %all-reduce.5.cloned.1.call-done = f32[256,256]{1,0:T(8,128)} async-done(((f32[256,256]{1,0:T(8,128)}), f32[256,256]{1,0:T(8,128)}) %all-reduce.5.cloned.1.call-update) | async-done | bytes 262160 | tf_op jit(solution)/shard_map/psum | solution.py:75
  513.2 66.1 %reduce-scatter.9.cloned.1.call-done = f32[256,256]{1,0:T(8,128)} async-done(((f32[4096,256]{1,0:T(8,128)}), f32[256,256]{1,0:T(8,128)}) %reduce-scatter.9.cloned.1.call-update) | async-done | bytes 262160 | tf_op jit(solution)/shard_map/reduce_scatter | solution.py:71
  580.8 67.3 %all-reduce.1 = (f32[256]{0:T(256)S(1)}, f32[256]{0:T(256)S(1)}) all-reduce(f32[256]{0:T(256)S(1)} %get-tuple-element.290, f32[256]{0:T(256)S(1)} %get-tuple-element.292), channel_id=1, replica_groups=mesh['row'=16,'col'=8] {'row','col'}, use_global_device_ids=true, to_apply=%region_5.6 | all-reduce | flops 512 | bytes 4096 | tf_op jit(solution)/shard_map/psum | solution.py:78
  648.8 31.3 %all-gather.7.cloned.1.call-done = bf16[4096,256]{1,0:T(8,128)(2,1)} async-done(((bf16[256,256]{1,0:T(8,128)(2,1)}), bf16[4096,256]{1,0:T(8,128)(2,1)}) %all-gather.7.cloned.1.call-update) | async-done | bytes 2097168 | tf_op jit(solution)/shard_map/all_gather | solution.py:62
  680.1 90.2 %while.45 = (s32[]{:T(128)}, f32[16,128,256]{2,0,1:T(8,128)S(1)}, s32[4,64]{1,0:T(4,128)S(1)}, bf16[4,64,128,128]{3,2,1,0:T(8,128)(2,1)}, s32[4,64]{1,0:T(4,128)...) while((s32[]{:T(128)}, f32[16,128,256]{2,0,1:T(8,128)S(1)}, ...), condition=%wide.region_7.8_spmd.clone, body=%wide.region_6.7_spmd.clone.sunk | while | flops 940574912 | bytes 35658084 | solution.py:29
  680.2 4.4 gather_fusion.1
  684.5 7.3 fusion.124
  691.8 10.8 select_add_fusion.9
  702.7 4.4 gather_fusion.1
  707.1 7.3 fusion.124
  714.4 10.8 select_add_fusion.9
  725.3 4.4 gather_fusion.1
  729.7 7.3 fusion.124
  736.9 10.8 select_add_fusion.9
  747.8 4.4 gather_fusion.1
  752.2 7.3 fusion.124
  759.5 10.8 select_add_fusion.9
  773.9 72.2 %reduce-scatter.7.cloned.1.call-done = f32[256,256]{1,0:T(8,128)} async-done(((f32[2048,256]{1,0:T(8,128)}), f32[256,256]{1,0:T(8,128)}) %reduce-scatter.7.cloned.1.call-update) | async-done | bytes 262160 | tf_op jit(solution)/shard_map/reduce_scatter | solution.py:70
  848.5 45.6 %all-gather.11.cloned.1.call-done = bf16[2048,256]{1,0:T(8,128)(2,1)} async-done(((bf16[256,256]{1,0:T(8,128)(2,1)}), bf16[2048,256]{1,0:T(8,128)(2,1)}) %all-gather.11.cloned.1.call-update) | async-done | bytes 1048592 | tf_op jit(solution)/shard_map/all_gather | solution.py:63
  894.1 102.2 %while.47 = (s32[]{:T(128)}, f32[32,128,256]{2,0,1:T(8,128)}, s32[4,64]{1,0:T(4,128)S(1)}, bf16[4,64,128,128]{2,3,1,0:T(8,128)(2,1)}, s32[4,64]{1,0:T(4,128)S(1)...) while((s32[]{:T(128)}, f32[32,128,256]{2,0,1:T(8,128)}, s32[4,64]{1,0:T(4,128)S(1)}, ...), condition=%wide.region_18.19_spmd.clone, body=%wide.region_17.18_spmd.clone.sunk | while | flops 1344277760 | bytes 39852388 | solution.py:29
  894.3 4.0 gather_fusion.3
  898.3 7.3 fusion.138
  905.6 13.2 %select_add_fusion.11 = f32[32,128,256]{2,0,1:T(8,128)} fusion(f32[32,128,256]{2,0,1:T(8,128)} %get-tuple-element.529, f32[64,128,256]{2,1,0:T(8,128)} %fusion.138, pred[]{:T(512)S(6)} %compare.22, s32[64]{0:T(128)S(1)} %fusion.139), kind=kOutput, calls=%fused_computation.57.clone.1 | convolution fusion | flops 807405568 | bytes 16777472 | tf_op jit(solution)/shard_map/while/body/eval_jaxpr/sn,sxp->nxp/dot_general | solution.py:25
  918.9 4.0 gather_fusion.3
  922.9 7.3 fusion.138
  930.2 14.4 %select_add_fusion.11 = f32[32,128,256]{2,0,1:T(8,128)} fusion(f32[32,128,256]{2,0,1:T(8,128)} %get-tuple-element.529, f32[64,128,256]{2,1,0:T(8,128)} %fusion.138, pred[]{:T(512)S(6)} %compare.22, s32[64]{0:T(128)S(1)} %fusion.139), kind=kOutput, calls=%fused_computation.57.clone.1 | convolution fusion | flops 807405568 | bytes 16777472 | tf_op jit(solution)/shard_map/while/body/eval_jaxpr/sn,sxp->nxp/dot_general | solution.py:25
  944.7 4.0 gather_fusion.3
  948.7 7.3 fusion.138
  956.0 14.4 %select_add_fusion.11 = f32[32,128,256]{2,0,1:T(8,128)} fusion(f32[32,128,256]{2,0,1:T(8,128)} %get-tuple-element.529, f32[64,128,256]{2,1,0:T(8,128)} %fusion.138, pred[]{:T(512)S(6)} %compare.22, s32[64]{0:T(128)S(1)} %fusion.139), kind=kOutput, calls=%fused_computation.57.clone.1 | convolution fusion | flops 807405568 | bytes 16777472 | tf_op jit(solution)/shard_map/while/body/eval_jaxpr/sn,sxp->nxp/dot_general | solution.py:25
  974.4 7.3 fusion.138
  981.7 14.4 %select_add_fusion.11 = f32[32,128,256]{2,0,1:T(8,128)} fusion(f32[32,128,256]{2,0,1:T(8,128)} %get-tuple-element.529, f32[64,128,256]{2,1,0:T(8,128)} %fusion.138, pred[]{:T(512)S(6)} %compare.22, s32[64]{0:T(128)S(1)} %fusion.139), kind=kOutput, calls=%fused_computation.57.clone.1 | convolution fusion | flops 807405568 | bytes 16777472 | tf_op jit(solution)/shard_map/while/body/eval_jaxpr/sn,sxp->nxp/dot_general | solution.py:25
  996.3 6.6 copy.28
  1003.9 37.4 %all-reduce.7.cloned.1.call-done = f32[256,256]{1,0:T(8,128)} async-done(((f32[256,256]{1,0:T(8,128)}), f32[256,256]{1,0:T(8,128)}) %all-reduce.7.cloned.1.call-update) | async-done | bytes 262160 | tf_op jit(solution)/shard_map/psum | solution.py:75
  1044.5 64.3 %reduce-scatter.11.cloned.1.call-done = f32[256,256]{1,0:T(8,128)} async-done(((f32[4096,256]{1,0:T(8,128)}), f32[256,256]{1,0:T(8,128)}) %reduce-scatter.11.cloned.1.call-update) | async-done | bytes 262160 | tf_op jit(solution)/shard_map/reduce_scatter | solution.py:71
  1110.2 67.3 %all-reduce = (f32[256]{0:T(256)S(1)}, f32[256]{0:T(256)S(1)}) all-reduce(f32[256]{0:T(256)S(1)} %get-tuple-element.294, f32[256]{0:T(256)S(1)} %get-tuple-element.296), channel_id=1, replica_groups=mesh['row'=16,'col'=8] {'row','col'}, use_global_device_ids=true, to_apply=%region_16.17 | all-reduce | flops 512 | bytes 4096 | tf_op jit(solution)/shard_map/psum | solution.py:78
  (116 shorter events, 46.1 us)
Async XLA Ops:
  29.1 5.4 copy-start.1
  29.1 5.4 copy-start.3
  29.1 5.4 copy-start.4
  29.1 120.6 %all-to-all-start.1 = ((bf16[256,128,128]{2,1,0:T(8,128)(2,1)}), bf16[256,128,128]{2,1,0:T(8,128)(2,1)}, u32[]{:S(2)}, u32[]{:S(2)}) async-start(bf16[256,128,128]{2,1,0:T(8,128)(2,1)} %param.14), calls=%async_computation.1 | async-start | bytes 16777216 | tf_op jit(solution)/shard_map/all_to_all | solution.py:43
  34.4 115.3 %all-gather.5.cloned.1.call-start = ((), (), s32[]{:S(2)}) async-start(), calls=%async_computation.6 | async-start | bytes 2228224 | tf_op jit(solution)/shard_map/all_gather | solution.py:62
  35.3 281.5 %reduce-scatter.5.cloned.1.call-start = ((), (), s32[]{:S(2)}) async-start(), calls=%async_computation.7 | async-start | bytes 2359296 | tf_op jit(solution)/shard_map/reduce_scatter | solution.py:70
  242.3 122.5 %all-gather.9.cloned.1.call-start = ((), (), s32[]{:S(2)}) async-start(), calls=%async_computation.11 | async-start | bytes 1179648 | tf_op jit(solution)/shard_map/all_gather | solution.py:63
  243.1 268.8 %all-reduce.5.cloned.1.call-start = ((), (), s32[]{:S(2)}) async-start(), calls=%async_computation.8 | async-start | bytes 524288 | tf_op jit(solution)/shard_map/psum | solution.py:75
  243.1 73.6 %copy-start.5 = (f32[256]{0:T(256)S(1)}, f32[256]{0:T(256)}, u32[]{:S(2)}) copy-start(f32[256]{0:T(256)} %param.18) | copy-start | bytes 3076
  319.1 260.2 %reduce-scatter.9.cloned.1.call-start = ((), (), s32[]{:S(2)}) async-start(), calls=%async_computation.12 | async-start | bytes 4456448 | tf_op jit(solution)/shard_map/reduce_scatter | solution.py:71
  473.3 38.6 %copy-start.2 = (f32[256,256]{1,0:T(8,128)S(1)}, f32[256,256]{1,0:T(8,128)}, u32[]{:S(2)}) copy-start(f32[256,256]{1,0:T(8,128)} %reduce-scatter.5.cloned.1.call-done) | copy-start | bytes 786436
  473.3 206.8 %all-gather.7.cloned.1.call-start = ((), (), s32[]{:S(2)}) async-start(), calls=%async_computation.9 | async-start | bytes 2228224 | tf_op jit(solution)/shard_map/all_gather | solution.py:62
  648.8 197.3 %reduce-scatter.7.cloned.1.call-start = ((), (), s32[]{:S(2)}) async-start(), calls=%async_computation.10 | async-start | bytes 2359296 | tf_op jit(solution)/shard_map/reduce_scatter | solution.py:70
  773.0 121.1 %all-gather.11.cloned.1.call-start = ((), (), s32[]{:S(2)}) async-start(), calls=%async_computation.14 | async-start | bytes 1179648 | tf_op jit(solution)/shard_map/all_gather | solution.py:63
  773.8 267.5 %all-reduce.7.cloned.1.call-start = ((), (), s32[]{:S(2)}) async-start(), calls=%async_computation.13 | async-start | bytes 524288 | tf_op jit(solution)/shard_map/psum | solution.py:75
  848.4 260.3 %reduce-scatter.11.cloned.1.call-start = ((), (), s32[]{:S(2)}) async-start(), calls=%async_computation.15 | async-start | bytes 4456448 | tf_op jit(solution)/shard_map/reduce_scatter | solution.py:71
  1002.9 0.9 copy-start
  1002.9 40.2 %copy-start.6 = (f32[256,256]{1,0:T(8,128)S(1)}, f32[256,256]{1,0:T(8,128)}, u32[]{:S(2)}) copy-start(f32[256,256]{1,0:T(8,128)} %reduce-scatter.7.cloned.1.call-done) | copy-start | bytes 786436
Sparse Core Ops, SparseCore 0:
  37.5 112.1 all-gather.4
  242.5 74.2 reduce-scatter.4
  319.7 45.0 all-gather.8
  370.0 141.8 all-reduce.4
  514.1 65.1 reduce-scatter.8
  648.9 31.1 all-gather.6
  773.1 72.9 reduce-scatter.6
  849.0 45.0 all-gather.10
  899.4 141.8 all-reduce.6
  1043.5 65.1 reduce-scatter.10
where the time goes:
time: 1200 us; the launch traced here: 1190 us
  waiting for transfers between devices  576 us (48%)
  matrix products  327 us (27%)
  blocking collectives  156 us (13%)
  local copies, waits for them, and re-layouts  99.6 us (8%)
  between operations  14.8 us (1%)
    dot_general x16, matrix products, accumulate(): jnp.einsum('sn,sxp->nxp', onehot, contrib, precision=lax.Precision.HIGHEST)  200 us
    all_gather x2, waiting for transfers between devices, local(): right_cols = lax.all_gather(right_bf, 'row', axis=0, tiled=True)  144 us
    psum x2, blocking collectives, local(): lax.psum((jnp.sum(right_rest * right_rest, axis=0), jnp.sum(left_rest * l...  135 us
    reduce_scatter x2, waiting for transfers between devices, local(): lax.psum_scatter(right_part, 'col', scatter_dimension=0, tiled=True)  134 us
    reduce_scatter x2, waiting for transfers between devices, local(): lax.psum_scatter(left_part, 'row', scatter_dimension=0, tiled=True)  130 us
    dot_general x16, matrix products, accumulate(): jnp.einsum(form, group_tiles, picked, preferred_element_type=jnp.float32)  117 us
    all_gather x2, waiting for transfers between devices, local(): left_rows = lax.all_gather(left_bf, 'col', axis=0, tiled=True)  90.7 us
    psum x2, waiting for transfers between devices, local(): project = lax.psum(local_proj, ('row', 'col')) / order_rows  75.9 us
  transfers between devices with their start and end apart: 11, of which 10 were waited for; matrix products, arithmetic and copies ran while one was open for 20% of the time, Pallas kernels for 0%

commit v1 on v0

--- a/solution.py
+++ b/solution.py
@@ -76,8 +76,11 @@
         right_rest = right_new - jnp.dot(right_vec, project, precision=lax.Precision.HIGHEST)
         left_rest = left_new - jnp.dot(left_vec, project.T, precision=lax.Precision.HIGHEST)
         right_sq, left_sq = lax.psum(
-            (jnp.sum(right_rest * right_rest, axis=0), jnp.sum(left_rest * left_rest, axis=0)),
-            ("row", "col"),
+            lax.psum(
+                (jnp.sum(right_rest * right_rest, axis=0), jnp.sum(left_rest * left_rest, axis=0)),
+                "row",
+            ),
+            "col",
         )
         right_vec = right_rest / jnp.sqrt(right_sq / order_rows + epsilon)[None, :]
         left_vec = left_rest / jnp.sqrt(left_sq / order_rows + epsilon)[None, :]

time: 1200 us -> 1170 us (0.975)
  blocking collectives: 156 us -> 120 us
    psum x2, blocking collectives: 135 us -> 59.3 us  [local(): lax.psum((jnp.sum(right_rest * right_rest, axis=0), jnp.sum(left_rest * l...]
    psum x0 -> x2, blocking collectives: none -> 40 us  [local(): lax.psum(lax.psum((jnp.sum(right_rest * right_rest, axis=0), jnp.sum(left...]
  transfers between devices with their start and end apart: 11 -> 11, of which waited for: 10 -> 10; matrix products, arithmetic and copies ran while one was open for 20% -> 21% of each run, Pallas kernels for 0% -> 0%
where the time goes in v1:
time: 1170 us; the launch traced here: 1150 us
  waiting for transfers between devices  579 us (49%)
  matrix products  327 us (28%)
  blocking collectives  120 us (10%)
  local copies, waits for them, and re-layouts  99.6 us (9%)
  between operations  14.8 us (1%)
    dot_general x16, matrix products, accumulate(): jnp.einsum('sn,sxp->nxp', onehot, contrib, precision=lax.Precision.HIGHEST)  200 us
    all_gather x2, waiting for transfers between devices, local(): right_cols = lax.all_gather(right_bf, 'row', axis=0, tiled=True)  147 us
    reduce_scatter x2, waiting for transfers between devices, local(): lax.psum_scatter(right_part, 'col', scatter_dimension=0, tiled=True)  133 us
    reduce_scatter x2, waiting for transfers between devices, local(): lax.psum_scatter(left_part, 'row', scatter_dimension=0, tiled=True)  130 us
    dot_general x16, matrix products, accumulate(): jnp.einsum(form, group_tiles, picked, preferred_element_type=jnp.float32)  117 us
    all_gather x2, waiting for transfers between devices, local(): left_rows = lax.all_gather(left_bf, 'col', axis=0, tiled=True)  90.7 us
    psum x2, waiting for transfers between devices, local(): project = lax.psum(local_proj, ('row', 'col')) / order_rows  76.1 us
    gather x16, local copies, waits for them, and re-layouts, accumulate(): picked = blocks[group_pick]  66.8 us
  transfers between devices with their start and end apart: 11, of which 10 were waited for; matrix products, arithmetic and copies ran while one was open for 21% of the time, Pallas kernels for 0%

profile of v1, /device:TPU:1, one launch (start us, length us, event | category | flops | bytes accessed | tf_op | source)
XLA Modules:
  0.0 1153.7 jit_solution(12476115966405141270)
XLA Ops:
  8.0 21.1 %all_to_all.17 = s32[128,2,1]{1,2,0:T(1,128)S(1)} all-to-all(s32[128,2,1]{1,2,0:T(1,128)S(1)} %bitcast.149), channel_id=1, replica_groups=mesh['row'=16,'col'=8] {'row','col'}, dimensions={0} | all-to-all | bytes 2048 | tf_op jit(solution)/shard_map/all_to_all | solution.py:44
  29.1 5.3 all-to-all-start.1
  36.8 112.9 %all-gather.5.cloned.1.call-done = bf16[4096,256]{1,0:T(8,128)(2,1)} async-done(((bf16[256,256]{1,0:T(8,128)(2,1)}), bf16[4096,256]{1,0:T(8,128)(2,1)}) %all-gather.5.cloned.1.call-update) | async-done | bytes 2097168 | tf_op jit(solution)/shard_map/all_gather | solution.py:62
  149.7 90.1 %while.44 = (s32[]{:T(128)}, f32[16,128,256]{2,0,1:T(8,128)S(1)}, s32[4,64]{1,0:T(4,128)S(1)}, bf16[4,64,128,128]{3,2,1,0:T(8,128)(2,1)}, s32[4,64]{1,0:T(4,128)...) while((s32[]{:T(128)}, f32[16,128,256]{2,0,1:T(8,128)S(1)}, ...), condition=%wide.region_1.2_spmd.clone, body=%wide.region_0.1_spmd.clone.sunk | while | flops 940574912 | bytes 35658084 | solution.py:29
  149.7 4.3 gather_fusion
  154.0 7.3 fusion.117
  161.3 10.8 select_add_fusion.8
  172.2 4.3 gather_fusion
  176.6 7.3 fusion.117
  183.9 10.8 select_add_fusion.8
  194.8 4.3 gather_fusion
  199.1 7.3 fusion.117
  206.4 10.8 select_add_fusion.8
  217.3 4.3 gather_fusion
  221.6 7.3 fusion.117
  228.9 10.8 select_add_fusion.8
  243.2 12.0 %copy.22 = bf16[256,128,128]{1,2,0:T(8,128)(2,1)} copy(bf16[256,128,128]{2,1,0:T(8,128)(2,1)} %all-to-all-done.1) | data formatting | bytes 16777216 | tf_op jit(solution)/shard_map/all_to_all | solution.py:43
  255.2 61.6 %reduce-scatter.5.cloned.1.call-done = f32[256,256]{1,0:T(8,128)} async-done(((f32[2048,256]{1,0:T(8,128)}), f32[256,256]{1,0:T(8,128)}) %reduce-scatter.5.cloned.1.call-update) | async-done | bytes 262160 | tf_op jit(solution)/shard_map/reduce_scatter | solution.py:70
  319.7 45.1 %all-gather.9.cloned.1.call-done = bf16[2048,256]{1,0:T(8,128)(2,1)} async-done(((bf16[256,256]{1,0:T(8,128)(2,1)}), bf16[2048,256]{1,0:T(8,128)(2,1)}) %all-gather.9.cloned.1.call-update) | async-done | bytes 1048592 | tf_op jit(solution)/shard_map/all_gather | solution.py:63
  364.8 101.8 %while.46 = (s32[]{:T(128)}, f32[32,128,256]{2,0,1:T(8,128)}, s32[4,64]{1,0:T(4,128)S(1)}, bf16[4,64,128,128]{2,3,1,0:T(8,128)(2,1)}, s32[4,64]{1,0:T(4,128)S(1)...) while((s32[]{:T(128)}, f32[32,128,256]{2,0,1:T(8,128)}, s32[4,64]{1,0:T(4,128)S(1)}, ...), condition=%wide.region_11.12_spmd.clone, body=%wide.region_10.11_spmd.clone.sunk | while | flops 1344277760 | bytes 39852388 | solution.py:29
  368.8 7.3 fusion.131
  376.1 13.3 %select_add_fusion.10 = f32[32,128,256]{2,0,1:T(8,128)} fusion(f32[32,128,256]{2,0,1:T(8,128)} %get-tuple-element.485, f32[64,128,256]{2,1,0:T(8,128)} %fusion.131, pred[]{:T(512)S(6)} %compare.21, s32[64]{0:T(128)S(1)} %fusion.132), kind=kOutput, calls=%fused_computation.40.clone.1 | convolution fusion | flops 807405568 | bytes 16777472 | tf_op jit(solution)/shard_map/while/body/eval_jaxpr/sn,sxp->nxp/dot_general | solution.py:25
  393.3 7.3 fusion.131
  400.6 14.5 %select_add_fusion.10 = f32[32,128,256]{2,0,1:T(8,128)} fusion(f32[32,128,256]{2,0,1:T(8,128)} %get-tuple-element.485, f32[64,128,256]{2,1,0:T(8,128)} %fusion.131, pred[]{:T(512)S(6)} %compare.21, s32[64]{0:T(128)S(1)} %fusion.132), kind=kOutput, calls=%fused_computation.40.clone.1 | convolution fusion | flops 807405568 | bytes 16777472 | tf_op jit(solution)/shard_map/while/body/eval_jaxpr/sn,sxp->nxp/dot_general | solution.py:25
  419.1 7.3 fusion.131
  426.4 14.4 %select_add_fusion.10 = f32[32,128,256]{2,0,1:T(8,128)} fusion(f32[32,128,256]{2,0,1:T(8,128)} %get-tuple-element.485, f32[64,128,256]{2,1,0:T(8,128)} %fusion.131, pred[]{:T(512)S(6)} %compare.21, s32[64]{0:T(128)S(1)} %fusion.132), kind=kOutput, calls=%fused_computation.40.clone.1 | convolution fusion | flops 807405568 | bytes 16777472 | tf_op jit(solution)/shard_map/while/body/eval_jaxpr/sn,sxp->nxp/dot_general | solution.py:25
  444.8 7.3 fusion.131
  452.1 14.4 %select_add_fusion.10 = f32[32,128,256]{2,0,1:T(8,128)} fusion(f32[32,128,256]{2,0,1:T(8,128)} %get-tuple-element.485, f32[64,128,256]{2,1,0:T(8,128)} %fusion.131, pred[]{:T(512)S(6)} %compare.21, s32[64]{0:T(128)S(1)} %fusion.132), kind=kOutput, calls=%fused_computation.40.clone.1 | convolution fusion | flops 807405568 | bytes 16777472 | tf_op jit(solution)/shard_map/while/body/eval_jaxpr/sn,sxp->nxp/dot_general | solution.py:25
  466.6 6.6 copy.27
  473.3 38.5 %all-reduce.7.cloned.1.call-done = f32[256,256]{1,0:T(8,128)} async-done(((f32[256,256]{1,0:T(8,128)}), f32[256,256]{1,0:T(8,128)}) %all-reduce.7.cloned.1.call-update) | async-done | bytes 262160 | tf_op jit(solution)/shard_map/psum | solution.py:75
  513.2 66.1 %reduce-scatter.9.cloned.1.call-done = f32[256,256]{1,0:T(8,128)} async-done(((f32[4096,256]{1,0:T(8,128)}), f32[256,256]{1,0:T(8,128)}) %reduce-scatter.9.cloned.1.call-update) | async-done | bytes 262160 | tf_op jit(solution)/shard_map/reduce_scatter | solution.py:71
  580.8 29.6 %all-reduce.1 = (f32[256]{0:T(256)S(1)}, f32[256]{0:T(256)S(1)}) all-reduce(f32[256]{0:T(256)S(1)} %get-tuple-element.294, f32[256]{0:T(256)S(1)} %get-tuple-element.296), channel_id=1, replica_groups=mesh['row'=16,'col'=8] {'row'}, use_global_device_ids=true, to_apply=%region_5.6 | all-reduce | flops 512 | bytes 4096 | tf_op jit(solution)/shard_map/psum | solution.py:79
  610.4 20.0 %all-reduce.3 = (f32[256]{0:T(256)S(1)}, f32[256]{0:T(256)S(1)}) all-reduce(f32[256]{0:T(256)S(1)} %get-tuple-element.281, f32[256]{0:T(256)S(1)} %get-tuple-element.282), channel_id=1, replica_groups=mesh['row'=16,'col'=8] {'col'}, use_global_device_ids=true, to_apply=%region_6.7 | all-reduce | flops 512 | bytes 4096 | tf_op jit(solution)/shard_map/psum | solution.py:78
  631.2 34.2 %all-gather.7.cloned.1.call-done = bf16[4096,256]{1,0:T(8,128)(2,1)} async-done(((bf16[256,256]{1,0:T(8,128)(2,1)}), bf16[4096,256]{1,0:T(8,128)(2,1)}) %all-gather.7.cloned.1.call-update) | async-done | bytes 2097168 | tf_op jit(solution)/shard_map/all_gather | solution.py:62
  665.4 90.2 %while.45 = (s32[]{:T(128)}, f32[16,128,256]{2,0,1:T(8,128)S(1)}, s32[4,64]{1,0:T(4,128)S(1)}, bf16[4,64,128,128]{3,2,1,0:T(8,128)(2,1)}, s32[4,64]{1,0:T(4,128)...) while((s32[]{:T(128)}, f32[16,128,256]{2,0,1:T(8,128)S(1)}, ...), condition=%wide.region_8.9_spmd.clone, body=%wide.region_7.8_spmd.clone.sunk | while | flops 940574912 | bytes 35658084 | solution.py:29
  665.4 4.4 gather_fusion.1
  669.8 7.3 fusion.124
  677.1 10.8 select_add_fusion.9
  687.9 4.4 gather_fusion.1
  692.3 7.3 fusion.124
  699.6 10.8 select_add_fusion.9
  710.5 4.4 gather_fusion.1
  714.9 7.3 fusion.124
  722.2 10.8 select_add_fusion.9
  733.1 4.4 gather_fusion.1
  737.4 7.3 fusion.124
  744.7 10.8 select_add_fusion.9
  759.3 71.9 %reduce-scatter.7.cloned.1.call-done = f32[256,256]{1,0:T(8,128)} async-done(((f32[2048,256]{1,0:T(8,128)}), f32[256,256]{1,0:T(8,128)}) %reduce-scatter.7.cloned.1.call-update) | async-done | bytes 262160 | tf_op jit(solution)/shard_map/reduce_scatter | solution.py:70
  833.6 45.6 %all-gather.11.cloned.1.call-done = bf16[2048,256]{1,0:T(8,128)(2,1)} async-done(((bf16[256,256]{1,0:T(8,128)(2,1)}), bf16[2048,256]{1,0:T(8,128)(2,1)}) %all-gather.11.cloned.1.call-update) | async-done | bytes 1048592 | tf_op jit(solution)/shard_map/all_gather | solution.py:63
  879.2 102.0 %while.47 = (s32[]{:T(128)}, f32[32,128,256]{2,0,1:T(8,128)}, s32[4,64]{1,0:T(4,128)S(1)}, bf16[4,64,128,128]{2,3,1,0:T(8,128)(2,1)}, s32[4,64]{1,0:T(4,128)S(1)...) while((s32[]{:T(128)}, f32[32,128,256]{2,0,1:T(8,128)}, s32[4,64]{1,0:T(4,128)S(1)}, ...), condition=%wide.region_21.22_spmd.clone, body=%wide.region_20.21_spmd.clone.sunk | while | flops 1344277760 | bytes 39852388 | solution.py:29
  883.3 7.3 fusion.138
  890.6 13.2 %select_add_fusion.11 = f32[32,128,256]{2,0,1:T(8,128)} fusion(f32[32,128,256]{2,0,1:T(8,128)} %get-tuple-element.533, f32[64,128,256]{2,1,0:T(8,128)} %fusion.138, pred[]{:T(512)S(6)} %compare.22, s32[64]{0:T(128)S(1)} %fusion.139), kind=kOutput, calls=%fused_computation.57.clone.1 | convolution fusion | flops 807405568 | bytes 16777472 | tf_op jit(solution)/shard_map/while/body/eval_jaxpr/sn,sxp->nxp/dot_general | solution.py:25
  903.8 4.0 gather_fusion.3
  907.8 7.3 fusion.138
  915.1 14.4 %select_add_fusion.11 = f32[32,128,256]{2,0,1:T(8,128)} fusion(f32[32,128,256]{2,0,1:T(8,128)} %get-tuple-element.533, f32[64,128,256]{2,1,0:T(8,128)} %fusion.138, pred[]{:T(512)S(6)} %compare.22, s32[64]{0:T(128)S(1)} %fusion.139), kind=kOutput, calls=%fused_computation.57.clone.1 | convolution fusion | flops 807405568 | bytes 16777472 | tf_op jit(solution)/shard_map/while/body/eval_jaxpr/sn,sxp->nxp/dot_general | solution.py:25
  933.6 7.3 fusion.138
  940.9 14.4 %select_add_fusion.11 = f32[32,128,256]{2,0,1:T(8,128)} fusion(f32[32,128,256]{2,0,1:T(8,128)} %get-tuple-element.533, f32[64,128,256]{2,1,0:T(8,128)} %fusion.138, pred[]{:T(512)S(6)} %compare.22, s32[64]{0:T(128)S(1)} %fusion.139), kind=kOutput, calls=%fused_computation.57.clone.1 | convolution fusion | flops 807405568 | bytes 16777472 | tf_op jit(solution)/shard_map/while/body/eval_jaxpr/sn,sxp->nxp/dot_general | solution.py:25
  959.3 7.3 fusion.138
  966.6 14.4 %select_add_fusion.11 = f32[32,128,256]{2,0,1:T(8,128)} fusion(f32[32,128,256]{2,0,1:T(8,128)} %get-tuple-element.533, f32[64,128,256]{2,1,0:T(8,128)} %fusion.138, pred[]{:T(512)S(6)} %compare.22, s32[64]{0:T(128)S(1)} %fusion.139), kind=kOutput, calls=%fused_computation.57.clone.1 | convolution fusion | flops 807405568 | bytes 16777472 | tf_op jit(solution)/shard_map/while/body/eval_jaxpr/sn,sxp->nxp/dot_general | solution.py:25
  981.3 6.6 copy.28
  988.8 37.6 %all-reduce.9.cloned.1.call-done = f32[256,256]{1,0:T(8,128)} async-done(((f32[256,256]{1,0:T(8,128)}), f32[256,256]{1,0:T(8,128)}) %all-reduce.9.cloned.1.call-update) | async-done | bytes 262160 | tf_op jit(solution)/shard_map/psum | solution.py:75
  1029.6 64.3 %reduce-scatter.11.cloned.1.call-done = f32[256,256]{1,0:T(8,128)} async-done(((f32[4096,256]{1,0:T(8,128)}), f32[256,256]{1,0:T(8,128)}) %reduce-scatter.11.cloned.1.call-update) | async-done | bytes 262160 | tf_op jit(solution)/shard_map/reduce_scatter | solution.py:71
  1095.3 29.6 %all-reduce = (f32[256]{0:T(256)S(1)}, f32[256]{0:T(256)S(1)}) all-reduce(f32[256]{0:T(256)S(1)} %get-tuple-element.298, f32[256]{0:T(256)S(1)} %get-tuple-element.300), channel_id=1, replica_groups=mesh['row'=16,'col'=8] {'row'}, use_global_device_ids=true, to_apply=%region_18.19 | all-reduce | flops 512 | bytes 4096 | tf_op jit(solution)/shard_map/psum | solution.py:79
  1125.0 20.0 %all-reduce.2 = (f32[256]{0:T(256)S(1)}, f32[256]{0:T(256)S(1)}) all-reduce(f32[256]{0:T(256)S(1)} %get-tuple-element.279, f32[256]{0:T(256)S(1)} %get-tuple-element.280), channel_id=1, replica_groups=mesh['row'=16,'col'=8] {'col'}, use_global_device_ids=true, to_apply=%region_19.20 | all-reduce | flops 512 | bytes 4096 | tf_op jit(solution)/shard_map/psum | solution.py:78
  (118 shorter events, 54.3 us)
Async XLA Ops:
  29.1 5.4 copy-start.1
  29.1 5.4 copy-start.3
  29.1 5.4 copy-start.4
  29.1 120.6 %all-to-all-start.1 = ((bf16[256,128,128]{2,1,0:T(8,128)(2,1)}), bf16[256,128,128]{2,1,0:T(8,128)(2,1)}, u32[]{:S(2)}, u32[]{:S(2)}) async-start(bf16[256,128,128]{2,1,0:T(8,128)(2,1)} %param.14), calls=%async_computation.1 | async-start | bytes 16777216 | tf_op jit(solution)/shard_map/all_to_all | solution.py:43
  34.4 115.3 %all-gather.5.cloned.1.call-start = ((), (), s32[]{:S(2)}) async-start(), calls=%async_computation.6 | async-start | bytes 2228224 | tf_op jit(solution)/shard_map/all_gather | solution.py:62
  35.3 281.5 %reduce-scatter.5.cloned.1.call-start = ((), (), s32[]{:S(2)}) async-start(), calls=%async_computation.7 | async-start | bytes 2359296 | tf_op jit(solution)/shard_map/reduce_scatter | solution.py:70
  242.4 122.4 %all-gather.9.cloned.1.call-start = ((), (), s32[]{:S(2)}) async-start(), calls=%async_computation.11 | async-start | bytes 1179648 | tf_op jit(solution)/shard_map/all_gather | solution.py:63
  243.1 268.8 %all-reduce.7.cloned.1.call-start = ((), (), s32[]{:S(2)}) async-start(), calls=%async_computation.8 | async-start | bytes 524288 | tf_op jit(solution)/shard_map/psum | solution.py:75
  243.2 73.6 %copy-start.5 = (f32[256]{0:T(256)S(1)}, f32[256]{0:T(256)}, u32[]{:S(2)}) copy-start(f32[256]{0:T(256)} %param.18) | copy-start | bytes 3076
  319.1 260.2 %reduce-scatter.9.cloned.1.call-start = ((), (), s32[]{:S(2)}) async-start(), calls=%async_computation.12 | async-start | bytes 4456448 | tf_op jit(solution)/shard_map/reduce_scatter | solution.py:71
  473.2 38.6 %copy-start.2 = (f32[256,256]{1,0:T(8,128)S(1)}, f32[256,256]{1,0:T(8,128)}, u32[]{:S(2)}) copy-start(f32[256,256]{1,0:T(8,128)} %reduce-scatter.5.cloned.1.call-done) | copy-start | bytes 786436
  473.3 192.1 %all-gather.7.cloned.1.call-start = ((), (), s32[]{:S(2)}) async-start(), calls=%async_computation.9 | async-start | bytes 2228224 | tf_op jit(solution)/shard_map/all_gather | solution.py:62
  631.1 200.1 %reduce-scatter.7.cloned.1.call-start = ((), (), s32[]{:S(2)}) async-start(), calls=%async_computation.10 | async-start | bytes 2359296 | tf_op jit(solution)/shard_map/reduce_scatter | solution.py:70
  758.2 121.0 %all-gather.11.cloned.1.call-start = ((), (), s32[]{:S(2)}) async-start(), calls=%async_computation.14 | async-start | bytes 1179648 | tf_op jit(solution)/shard_map/all_gather | solution.py:63
  759.0 267.4 %all-reduce.9.cloned.1.call-start = ((), (), s32[]{:S(2)}) async-start(), calls=%async_computation.13 | async-start | bytes 524288 | tf_op jit(solution)/shard_map/psum | solution.py:75
  833.6 260.3 %reduce-scatter.11.cloned.1.call-start = ((), (), s32[]{:S(2)}) async-start(), calls=%async_computation.15 | async-start | bytes 4456448 | tf_op jit(solution)/shard_map/reduce_scatter | solution.py:71
  987.9 0.9 copy-start
  987.9 40.4 %copy-start.6 = (f32[256,256]{1,0:T(8,128)S(1)}, f32[256,256]{1,0:T(8,128)}, u32[]{:S(2)}) copy-start(f32[256,256]{1,0:T(8,128)} %reduce-scatter.7.cloned.1.call-done) | copy-start | bytes 786436
Sparse Core Ops, SparseCore 0:
  37.5 112.1 all-gather.4
  242.5 74.2 reduce-scatter.4
  319.7 45.0 all-gather.8
  370.0 141.8 all-reduce.6
  514.1 65.1 reduce-scatter.8
  631.2 34.0 all-gather.6
  758.3 72.8 reduce-scatter.6
  834.1 45.0 all-gather.10
  884.5 141.8 all-reduce.8
  1028.7 65.1 reduce-scatter.10
